TPU v7x, 32 devices: a whole 2x2x4 slice. The times are simulated.
32 devices in a mesh: horiz: 8 (over z, y), lev: 4 (over x, core).
Axes of the slice: x: 2, y: 2, z: 4, core: 2. Of those that a mesh axis runs over, the one named last changes fastest.
Arguments:
- control: float32 [64, 32, 4096], P('lev', None, 'horiz'), may hold values from -6 to 6
- members: bfloat16 [64, 4, 32, 4096], P('lev', None, None, 'horiz'), may hold values from -6 to 6
- extinction: float32 [4], replicated, may hold values from 0.5 to 2
- kernels: bfloat16 [4096, 64, 128], P('horiz', 'lev'), may hold values from 0 to 1
- innovation: bfloat16 [4096, 128], P('horiz'), may hold values from -16 to 16
- obs_weight: bfloat16 [4096, 128], P('horiz'), may hold values from 0.25 to 4
- owners: int32 [4096, 1], P('horiz'), may hold values from 0 to 7; in each aligned block of 512 rows (0 to 511, 512 to 1023, ...) at most 128 rows name the same one
- pixel_columns: int32 [4096, 128], P('horiz'), may hold values from 0 to 511
- pixel_counts: int32 [4096], P('horiz'), may hold values from 1 to 128
Outputs:
- gradient: float32 [64, 32, 4096], P('lev', None, 'horiz')
Inputs may be any that keep to these rules, and one draw needn't show every extreme that they name: `owners`: among the 512 blocks of one index of horiz, no owner is named more than 128 times, and in some index's blocks one owner is named exactly 128 times.
All inputs are finite; a program needn't handle non-finite values.
Results may differ from a plain program's by a relative error of at most 0.0037.
Values may be sent and summed in bfloat16 or wider, within the bound.
A program may use at most 128 MiB of HBM per device.

v0:
```python
import math
import jax
import jax.numpy as jnp
from jax import lax
from jax.sharding import PartitionSpec as P

LEV = 64
HALF = 4


def with_halo(value, sides, width):
    for axis, dim in sides:
        devices, length = (lax.axis_size(axis), value.shape[dim])
        up = [(i, (i + 1) % devices) for i in range(devices - 1)]
        down = [(j, i) for i, j in up]
        last = lax.slice_in_dim(value, length - width, length, axis=dim)
        first = lax.slice_in_dim(value, 0, width, axis=dim)
        before = lax.ppermute(last, axis, up)
        after = lax.ppermute(first, axis, down)
        value = jnp.concatenate([before, value, after], axis=dim)
    return value


def level_matrix():
    index_levels = jnp.arange(LEV, dtype=jnp.float32)
    spread = LEV / 8.0
    distance = index_levels[:, None] - index_levels[None, :]
    matrix = jnp.exp(-distance * distance / (2.0 * spread * spread)) / (2.5066283 * spread)
    return matrix.astype(jnp.bfloat16)


def column_taps():
    offsets = jnp.arange(2 * HALF + 1, dtype=jnp.float32) - HALF
    spread = HALF / 2.0
    weights = jnp.exp(-offsets * offsets / (2.0 * spread * spread))
    return weights / jnp.sum(weights)


def smooth_columns(values):
    tap_weights = column_taps()
    span = values.shape[2]
    padded = with_halo(values, (("horiz", 2),), HALF)
    running = jnp.zeros(values.shape, jnp.float32)
    for offset in range(2 * HALF + 1):
        running = running + tap_weights[offset] * padded[:, :, offset : offset + span]
    return running


def evolve_pixels(kernel_rows, picked):
    return jnp.sum(kernel_rows.astype(jnp.float32) * picked, axis=1)


def pixel_misfit(evolved, innov_rows, weight_rows, count_rows):
    pixel_width = evolved.shape[1]
    live_pixels = jnp.arange(pixel_width, dtype=jnp.int32)[None, :] < count_rows[:, None]
    return jnp.where(
        live_pixels,
        weight_rows.astype(jnp.float32) * (evolved - innov_rows.astype(jnp.float32)),
        0.0,
    )


def column_onehot(column_block, col_count):
    return (
        jnp.arange(col_count, dtype=jnp.int32)[:, None, None] == column_block[None, :, :]
    ).astype(jnp.float32)


def body(
    control,
    members,
    extinction,
    kernels,
    innovation,
    obs_weight,
    owners,
    pixel_columns,
    pixel_counts,
):
    lev_local, mem_count, col_count = control.shape
    level_loc = level_matrix()
    first_level = lax.axis_index("lev") * lev_local
    mine_rows = lax.dynamic_slice_in_dim(level_loc, first_level, lev_local, 0)
    mine_cols = lax.dynamic_slice_in_dim(level_loc, first_level, lev_local, 1)
    scale = 1.0 / math.sqrt(mem_count)
    control_b = control.astype(jnp.bfloat16)
    section = mine_rows
    vertical = jnp.einsum(
        "ab,bmc->amc",
        section,
        lax.all_gather(control_b, "lev", axis=0, tiled=True),
        preferred_element_type=jnp.float32,
    )
    increment = smooth_columns(vertical)
    mixed = extinction[0] * members[:, 0].astype(jnp.float32)
    for species in range(1, members.shape[1]):
        mixed = mixed + extinction[species] * members[:, species].astype(jnp.float32)
    column_field = jnp.sum(mixed * increment, axis=1) * scale
    owner_ids = owners[:, 0]
    horiz_count = lax.axis_size("horiz")
    blocks_local = owner_ids.shape[0]
    pixel_width = pixel_columns.shape[1]
    capacity = max(2, 2 * (blocks_local // horiz_count))
    total_slots = horiz_count * capacity
    owner_range = jnp.arange(horiz_count, dtype=jnp.int32)
    belongs = (owner_ids[:, None] == owner_range[None, :]).astype(jnp.float32)
    block_range = jnp.arange(blocks_local, dtype=jnp.int32)
    strictly_lower = (block_range[:, None] > block_range[None, :]).astype(jnp.float32)
    earlier = jnp.dot(strictly_lower, belongs, precision=lax.Precision.HIGHEST)
    slot_index = jnp.sum(earlier * belongs, axis=1).astype(jnp.int32)
    target_slot = owner_ids * capacity + slot_index
    placement = jnp.arange(total_slots, dtype=jnp.int32)[:, None] == target_slot[None, :]
    place_half = placement.astype(jnp.bfloat16)
    kernel_buf = (
        jnp.dot(place_half, kernels.reshape(blocks_local, -1), preferred_element_type=jnp.float32)
        .astype(jnp.bfloat16)
        .reshape((total_slots,) + kernels.shape[1:])
    )
    paired = jnp.stack([innovation, obs_weight], 1).reshape(blocks_local, -1)
    value_buf = (
        jnp.dot(place_half, paired, preferred_element_type=jnp.float32)
        .astype(jnp.bfloat16)
        .reshape(total_slots, 2, pixel_width)
    )
    index_rows = jnp.concatenate([pixel_columns, pixel_counts[:, None]], 1).astype(jnp.float32)
    index_buf = jnp.dot(
        placement.astype(jnp.float32), index_rows, precision=lax.Precision.HIGHEST
    ).astype(jnp.int32)
    column_buf = index_buf[:, :pixel_width]
    count_buf = index_buf[:, pixel_width]
    kernel_in, value_in = (
        lax.all_to_all(kernel_buf, "horiz", split_axis=0, concat_axis=0, tiled=True),
        lax.all_to_all(value_buf, "horiz", split_axis=0, concat_axis=0, tiled=True),
    )
    column_in, count_in = (
        lax.all_to_all(column_buf, "horiz", split_axis=0, concat_axis=0, tiled=True),
        lax.all_to_all(count_buf, "horiz", split_axis=0, concat_axis=0, tiled=True),
    )
    slot_group = math.gcd(total_slots, 64)
    group_count = total_slots // slot_group
    kernel_groups = kernel_in.reshape(group_count, slot_group, lev_local, pixel_width)
    column_groups = column_in.reshape(group_count, slot_group, pixel_width)

    def forward_group(operands):
        kernel_block, column_block = operands
        onehot = column_onehot(column_block, col_count)
        picked = jnp.einsum("ac,cgp->gap", column_field, onehot, precision=lax.Precision.HIGHEST)
        return evolve_pixels(kernel_block, picked)

    local_sums = lax.map(forward_group, (kernel_groups, column_groups)).reshape(
        total_slots, pixel_width
    )
    evolved = lax.psum(local_sums, "lev")
    misfit = pixel_misfit(evolved, value_in[:, 0], value_in[:, 1], count_in)
    misfit_groups = misfit.reshape(group_count, slot_group, pixel_width)

    def adjoint_group(running, operands):
        kernel_block, column_block, misfit_block = operands
        onehot = column_onehot(column_block, col_count)
        contrib = kernel_block.astype(jnp.float32) * misfit_block[:, None, :]
        return (
            running + jnp.einsum("gap,cgp->ac", contrib, onehot, precision=lax.Precision.HIGHEST),
            None,
        )

    field_grad, unused = lax.scan(
        adjoint_group,
        jnp.zeros((lev_local, col_count), jnp.float32),
        (kernel_groups, column_groups, misfit_groups),
    )
    member_grad = mixed * field_grad[:, None, :] * scale
    smoothed_b = smooth_columns(member_grad).astype(jnp.bfloat16)
    section = mine_cols
    adjoint_field = jnp.einsum(
        "ba,bmc->amc",
        section,
        lax.all_gather(smoothed_b, "lev", axis=0, tiled=True),
        preferred_element_type=jnp.float32,
    )
    return control + adjoint_field


def solution(mesh):
    placed = (
        P("lev", None, "horiz"),
        P("lev", None, None, "horiz"),
        P(),
        P("horiz", "lev", None),
        P("horiz", None),
        P("horiz", None),
        P("horiz", None),
        P("horiz", None),
        P("horiz"),
    )
    return jax.shard_map(
        body, mesh=mesh, in_specs=placed, out_specs=P("lev", None, "horiz"), check_vma=False
    )
```

profile of v0, /device:TPU:0, one launch (start us, length us, event | category | flops | bytes accessed | tf_op | source)
XLA Modules:
  0.0 520.4 jit_solution(10034451160661777724)
XLA Ops:
  12.4 7.3 %all-to-all-start.3 = ((s32[8,128,128]{1,2,0:T(8,128)}), s32[8,128,128]{1,2,0:T(8,128)S(1)}, u32[]{:S(2)}, u32[]{:S(2)}) async-start(s32[8,128,128]{1,2,0:T(8,128)} %copy_bitcast_fusion), calls=%async_computation.3 | async-start | bytes 1048576 | tf_op jit(solution)/shard_map/all_to_all | solution.py:136
  25.5 8.7 %all-to-all-done.3 = s32[8,128,128]{1,2,0:T(8,128)S(1)} async-done(((s32[8,128,128]{1,2,0:T(8,128)}), s32[8,128,128]{1,2,0:T(8,128)S(1)}, u32[]{:S(2)}, u32[]{:S(2)}) %all-to-all-start.3) | async-done | bytes 524320 | tf_op jit(solution)/shard_map/all_to_all | solution.py:136
  47.7 18.3 %all-gather.3.cloned.1.call-done = bf16[64,32,512]{2,0,1:T(8,128)(2,1)} async-done(((bf16[16,32,512]{2,0,1:T(8,128)(2,1)}), bf16[64,32,512]{2,0,1:T(8,128)(2,1)}) %all-gather.3.cloned.1.call-update) | async-done | bytes 2097168 | tf_op jit(solution)/shard_map/all_gather | solution.py:91
  70.1 5.3 %collective-permute-start = (f32[16,32,4]{2,0,1:T(8,128)S(1)}, f32[16,32,4]{2,0,1:T(8,128)}, u32[]{:S(2)}, u32[]{:S(2)}) collective-permute-start(f32[16,32,4]{2,0,1:T(8,128)S(1)} %get-tuple-element.107), channel_id=1, source_target_pairs={{0,4},{4,8},{8,12},{12,16},{16,20},{20,24},{24,28},{1,5},{5,9},{9,... | collective-permute-start | bytes 24584 | tf_op jit(solution)/shard_map/ppermute | solution.py:18
  78.2 12.2 %collective-permute-done.1 = f32[16,32,4]{2,0,1:T(8,128)} collective-permute-done((f32[16,32,4]{2,0,1:T(8,128)}, f32[16,32,4]{2,0,1:T(8,128)}, u32[]{:S(2)}, u32[]{:S(2)}) %collective-permute-start.1) | collective-permute-done | bytes 8224 | tf_op jit(solution)/shard_map/ppermute | solution.py:19
  90.4 13.0 %fusion.47 = (f32[16,512]{1,0:T(8,128)S(1)}, f32[16,1,32,512]{3,0,2,1:T(8,128)S(1)}) fusion(f32[16,32,512]{2,0,1:T(8,128)S(1)} %fusion.82, f32[16,32,4]{2,0,1:T(8,128)} %collective-permute-done.1, f32[16,32,4]{2,0,1:T(8,128)} %collective-permute-done, f32[]{:T(128)} %bitcast.32, f32[]{:T(128)} %bitcast.31, f32[]{:T(128)} %bitcast.30, f32[]{:T(128)} %bitcast.29, ...), kind=kLoop, calls=%fused_computation.82 | loop fusion | flops 9953280 | bytes 4243508 | tf_op jit(solution)/shard_map/reduce_sum | solution.py:98
  103.5 30.8 %all-to-all-done = bf16[1024,16,128]{2,1,0:T(8,128)(2,1)} async-done(((bf16[1024,16,128]{2,1,0:T(8,128)(2,1)}), bf16[1024,16,128]{2,1,0:T(8,128)(2,1)}, u32[]{:S(2)}, u32[]{:S(2)}) %all-to-all-start) | async-done | bytes 4194336 | tf_op jit(solution)/shard_map/all_to_all | solution.py:132
  134.3 19.4 %all-to-all-start.2 = ((bf16[1024,2,128]{2,1,0:T(2,128)(2,1)}), bf16[1024,2,128]{2,1,0:T(2,128)(2,1)S(1)}, u32[]{:S(2)}, u32[]{:S(2)}) async-start(bf16[1024,2,128]{2,1,0:T(2,128)(2,1)} %copy.58), calls=%async_computation.2 | async-start | bytes 1048576 | tf_op jit(solution)/shard_map/all_to_all | solution.py:133
  154.0 123.3 %while.21 = (s32[]{:T(128)}, f32[16,64,128]{2,1,0:T(8,128)}, bf16[16,64,16,128]{3,2,1,0:T(8,128)(2,1)}, s32[16,64,128]{2,1,0:T(8,128)}, f32[16,512]{1,0:T(8,128)S(1)}, /*index=5*/s32[]{:T(128)}) while((s32[]{:T(128)}, f32[16,64,128]{2,1,0:T(8,128)}, bf16[16,64,16,128]{3,2,1,0:T(8,128)(2,1)}, s32[16,64,128]{2,1,0:T(8,128)}, ...), condition=%wide.region_5.6_spmd, body=%wide.region_3.5_spmd.sunk | while | flops 809885696 | bytes 491609 | solution.py:150
  154.7 6.3 %fusion.104 = f32[64,128]{1,0:T(8,128)S(1)} fusion(s32[64,128]{1,0:T(8,128)S(1)} %dynamic-slice_bitcast_fusion.6, bf16[16,64,16,128]{3,2,1,0:T(8,128)(2,1)} %get-tuple-element.200, s32[]{:T(128)S(6)} %copy.98, f32[16,512]{1,0:T(8,128)S(1)} %get-tuple-element.202), kind=kOutput, calls=%fused_computation.5.clone.1 | convolution fusion | flops 809885696 | bytes 360452 | tf_op jit(solution)/shard_map/while/body/eval_jaxpr/ac,cgp->gap/dot_general | solution.py:147
  162.4 6.3 %fusion.104 = f32[64,128]{1,0:T(8,128)S(1)} fusion(s32[64,128]{1,0:T(8,128)S(1)} %dynamic-slice_bitcast_fusion.6, bf16[16,64,16,128]{3,2,1,0:T(8,128)(2,1)} %get-tuple-element.200, s32[]{:T(128)S(6)} %copy.98, f32[16,512]{1,0:T(8,128)S(1)} %get-tuple-element.202), kind=kOutput, calls=%fused_computation.5.clone.1 | convolution fusion | flops 809885696 | bytes 360452 | tf_op jit(solution)/shard_map/while/body/eval_jaxpr/ac,cgp->gap/dot_general | solution.py:147
  170.1 6.3 %fusion.104 = f32[64,128]{1,0:T(8,128)S(1)} fusion(s32[64,128]{1,0:T(8,128)S(1)} %dynamic-slice_bitcast_fusion.6, bf16[16,64,16,128]{3,2,1,0:T(8,128)(2,1)} %get-tuple-element.200, s32[]{:T(128)S(6)} %copy.98, f32[16,512]{1,0:T(8,128)S(1)} %get-tuple-element.202), kind=kOutput, calls=%fused_computation.5.clone.1 | convolution fusion | flops 809885696 | bytes 360452 | tf_op jit(solution)/shard_map/while/body/eval_jaxpr/ac,cgp->gap/dot_general | solution.py:147
  177.9 6.3 %fusion.104 = f32[64,128]{1,0:T(8,128)S(1)} fusion(s32[64,128]{1,0:T(8,128)S(1)} %dynamic-slice_bitcast_fusion.6, bf16[16,64,16,128]{3,2,1,0:T(8,128)(2,1)} %get-tuple-element.200, s32[]{:T(128)S(6)} %copy.98, f32[16,512]{1,0:T(8,128)S(1)} %get-tuple-element.202), kind=kOutput, calls=%fused_computation.5.clone.1 | convolution fusion | flops 809885696 | bytes 360452 | tf_op jit(solution)/shard_map/while/body/eval_jaxpr/ac,cgp->gap/dot_general | solution.py:147
  185.6 6.3 %fusion.104 = f32[64,128]{1,0:T(8,128)S(1)} fusion(s32[64,128]{1,0:T(8,128)S(1)} %dynamic-slice_bitcast_fusion.6, bf16[16,64,16,128]{3,2,1,0:T(8,128)(2,1)} %get-tuple-element.200, s32[]{:T(128)S(6)} %copy.98, f32[16,512]{1,0:T(8,128)S(1)} %get-tuple-element.202), kind=kOutput, calls=%fused_computation.5.clone.1 | convolution fusion | flops 809885696 | bytes 360452 | tf_op jit(solution)/shard_map/while/body/eval_jaxpr/ac,cgp->gap/dot_general | solution.py:147
  193.3 6.3 %fusion.104 = f32[64,128]{1,0:T(8,128)S(1)} fusion(s32[64,128]{1,0:T(8,128)S(1)} %dynamic-slice_bitcast_fusion.6, bf16[16,64,16,128]{3,2,1,0:T(8,128)(2,1)} %get-tuple-element.200, s32[]{:T(128)S(6)} %copy.98, f32[16,512]{1,0:T(8,128)S(1)} %get-tuple-element.202), kind=kOutput, calls=%fused_computation.5.clone.1 | convolution fusion | flops 809885696 | bytes 360452 | tf_op jit(solution)/shard_map/while/body/eval_jaxpr/ac,cgp->gap/dot_general | solution.py:147
  201.0 6.3 %fusion.104 = f32[64,128]{1,0:T(8,128)S(1)} fusion(s32[64,128]{1,0:T(8,128)S(1)} %dynamic-slice_bitcast_fusion.6, bf16[16,64,16,128]{3,2,1,0:T(8,128)(2,1)} %get-tuple-element.200, s32[]{:T(128)S(6)} %copy.98, f32[16,512]{1,0:T(8,128)S(1)} %get-tuple-element.202), kind=kOutput, calls=%fused_computation.5.clone.1 | convolution fusion | flops 809885696 | bytes 360452 | tf_op jit(solution)/shard_map/while/body/eval_jaxpr/ac,cgp->gap/dot_general | solution.py:147
  208.7 6.3 %fusion.104 = f32[64,128]{1,0:T(8,128)S(1)} fusion(s32[64,128]{1,0:T(8,128)S(1)} %dynamic-slice_bitcast_fusion.6, bf16[16,64,16,128]{3,2,1,0:T(8,128)(2,1)} %get-tuple-element.200, s32[]{:T(128)S(6)} %copy.98, f32[16,512]{1,0:T(8,128)S(1)} %get-tuple-element.202), kind=kOutput, calls=%fused_computation.5.clone.1 | convolution fusion | flops 809885696 | bytes 360452 | tf_op jit(solution)/shard_map/while/body/eval_jaxpr/ac,cgp->gap/dot_general | solution.py:147
  216.4 6.3 %fusion.104 = f32[64,128]{1,0:T(8,128)S(1)} fusion(s32[64,128]{1,0:T(8,128)S(1)} %dynamic-slice_bitcast_fusion.6, bf16[16,64,16,128]{3,2,1,0:T(8,128)(2,1)} %get-tuple-element.200, s32[]{:T(128)S(6)} %copy.98, f32[16,512]{1,0:T(8,128)S(1)} %get-tuple-element.202), kind=kOutput, calls=%fused_computation.5.clone.1 | convolution fusion | flops 809885696 | bytes 360452 | tf_op jit(solution)/shard_map/while/body/eval_jaxpr/ac,cgp->gap/dot_general | solution.py:147
  224.1 6.3 %fusion.104 = f32[64,128]{1,0:T(8,128)S(1)} fusion(s32[64,128]{1,0:T(8,128)S(1)} %dynamic-slice_bitcast_fusion.6, bf16[16,64,16,128]{3,2,1,0:T(8,128)(2,1)} %get-tuple-element.200, s32[]{:T(128)S(6)} %copy.98, f32[16,512]{1,0:T(8,128)S(1)} %get-tuple-element.202), kind=kOutput, calls=%fused_computation.5.clone.1 | convolution fusion | flops 809885696 | bytes 360452 | tf_op jit(solution)/shard_map/while/body/eval_jaxpr/ac,cgp->gap/dot_general | solution.py:147
  231.8 6.3 %fusion.104 = f32[64,128]{1,0:T(8,128)S(1)} fusion(s32[64,128]{1,0:T(8,128)S(1)} %dynamic-slice_bitcast_fusion.6, bf16[16,64,16,128]{3,2,1,0:T(8,128)(2,1)} %get-tuple-element.200, s32[]{:T(128)S(6)} %copy.98, f32[16,512]{1,0:T(8,128)S(1)} %get-tuple-element.202), kind=kOutput, calls=%fused_computation.5.clone.1 | convolution fusion | flops 809885696 | bytes 360452 | tf_op jit(solution)/shard_map/while/body/eval_jaxpr/ac,cgp->gap/dot_general | solution.py:147
  239.5 6.3 %fusion.104 = f32[64,128]{1,0:T(8,128)S(1)} fusion(s32[64,128]{1,0:T(8,128)S(1)} %dynamic-slice_bitcast_fusion.6, bf16[16,64,16,128]{3,2,1,0:T(8,128)(2,1)} %get-tuple-element.200, s32[]{:T(128)S(6)} %copy.98, f32[16,512]{1,0:T(8,128)S(1)} %get-tuple-element.202), kind=kOutput, calls=%fused_computation.5.clone.1 | convolution fusion | flops 809885696 | bytes 360452 | tf_op jit(solution)/shard_map/while/body/eval_jaxpr/ac,cgp->gap/dot_general | solution.py:147
  247.2 6.3 %fusion.104 = f32[64,128]{1,0:T(8,128)S(1)} fusion(s32[64,128]{1,0:T(8,128)S(1)} %dynamic-slice_bitcast_fusion.6, bf16[16,64,16,128]{3,2,1,0:T(8,128)(2,1)} %get-tuple-element.200, s32[]{:T(128)S(6)} %copy.98, f32[16,512]{1,0:T(8,128)S(1)} %get-tuple-element.202), kind=kOutput, calls=%fused_computation.5.clone.1 | convolution fusion | flops 809885696 | bytes 360452 | tf_op jit(solution)/shard_map/while/body/eval_jaxpr/ac,cgp->gap/dot_general | solution.py:147
  254.9 6.3 %fusion.104 = f32[64,128]{1,0:T(8,128)S(1)} fusion(s32[64,128]{1,0:T(8,128)S(1)} %dynamic-slice_bitcast_fusion.6, bf16[16,64,16,128]{3,2,1,0:T(8,128)(2,1)} %get-tuple-element.200, s32[]{:T(128)S(6)} %copy.98, f32[16,512]{1,0:T(8,128)S(1)} %get-tuple-element.202), kind=kOutput, calls=%fused_computation.5.clone.1 | convolution fusion | flops 809885696 | bytes 360452 | tf_op jit(solution)/shard_map/while/body/eval_jaxpr/ac,cgp->gap/dot_general | solution.py:147
  262.6 6.3 %fusion.104 = f32[64,128]{1,0:T(8,128)S(1)} fusion(s32[64,128]{1,0:T(8,128)S(1)} %dynamic-slice_bitcast_fusion.6, bf16[16,64,16,128]{3,2,1,0:T(8,128)(2,1)} %get-tuple-element.200, s32[]{:T(128)S(6)} %copy.98, f32[16,512]{1,0:T(8,128)S(1)} %get-tuple-element.202), kind=kOutput, calls=%fused_computation.5.clone.1 | convolution fusion | flops 809885696 | bytes 360452 | tf_op jit(solution)/shard_map/while/body/eval_jaxpr/ac,cgp->gap/dot_general | solution.py:147
  270.3 6.3 %fusion.104 = f32[64,128]{1,0:T(8,128)S(1)} fusion(s32[64,128]{1,0:T(8,128)S(1)} %dynamic-slice_bitcast_fusion.6, bf16[16,64,16,128]{3,2,1,0:T(8,128)(2,1)} %get-tuple-element.200, s32[]{:T(128)S(6)} %copy.98, f32[16,512]{1,0:T(8,128)S(1)} %get-tuple-element.202), kind=kOutput, calls=%fused_computation.5.clone.1 | convolution fusion | flops 809885696 | bytes 360452 | tf_op jit(solution)/shard_map/while/body/eval_jaxpr/ac,cgp->gap/dot_general | solution.py:147
  277.3 5.8 %all-to-all-start.1 = ((s32[8,128,1]{1,2,0:T(1,128)}), s32[8,128,1]{1,2,0:T(1,128)S(1)}, u32[]{:S(2)}, u32[]{:S(2)}) async-start(s32[8,128,1]{1,2,0:T(1,128)} %slice_bitcast_fusion.1), calls=%async_computation.1 | async-start | bytes 8192 | tf_op jit(solution)/shard_map/all_to_all | solution.py:137
  289.5 22.2 %all-reduce.2.cloned.1.call-done = f32[1024,128]{1,0:T(8,128)} async-done(((f32[1024,128]{1,0:T(8,128)}), f32[1024,128]{1,0:T(8,128)}) %all-reduce.2.cloned.1.call-update) | async-done | bytes 524304 | tf_op jit(solution)/shard_map/psum | solution.py:153
  313.1 147.6 %while.22 = (s32[]{:T(128)}, f32[16,512]{1,0:T(8,128)S(1)}, bf16[16,64,16,128]{3,2,1,0:T(8,128)(2,1)}, f32[16,64,128]{2,1,0:T(8,128)S(1)}, s32[16,64,128]{2,1,0:T(8,128)}, /*index=5*/s32[]{:T(128)}, s32[]{:T(128)}) while((s32[]{:T(128)}, f32[16,512]{1,0:T(8,128)S(1)}, bf16[16,64,16,128]{3,2,1,0:T(8,128)(2,1)}, ...), condition=%wide.region_8.9_spmd.clone, body=%wide.region_7.8_spmd.clone.sunk | while | flops 809779200 | bytes 524395 | solution.py:166
  313.9 8.4 %fusion.105 = f32[16,512]{1,0:T(8,128)S(1)} fusion(s32[64,128]{1,0:T(8,128)S(1)} %dynamic-slice_bitcast_fusion.7, f32[64,128]{1,0:T(8,128)S(1)} %dynamic-slice_bitcast_fusion.8, bf16[16,64,16,128]{3,2,1,0:T(8,128)(2,1)} %get-tuple-element.220, s32[]{:T(128)S(6)} %copy.105, f32[16,512]{1,0:T(8,128)S(1)} %get-tuple-element.212, pred[]{:T(512)S(6)} %compare.3), kind=kOutput, calls=%fused_computation.13.clone.1 | convolution fusion | flops 809779200 | bytes 393221 | tf_op jit(solution)/shard_map/while/body/eval_jaxpr/gap,cgp->ac/dot_general | solution.py:162
  323.2 8.4 %fusion.105 = f32[16,512]{1,0:T(8,128)S(1)} fusion(s32[64,128]{1,0:T(8,128)S(1)} %dynamic-slice_bitcast_fusion.7, f32[64,128]{1,0:T(8,128)S(1)} %dynamic-slice_bitcast_fusion.8, bf16[16,64,16,128]{3,2,1,0:T(8,128)(2,1)} %get-tuple-element.220, s32[]{:T(128)S(6)} %copy.105, f32[16,512]{1,0:T(8,128)S(1)} %get-tuple-element.212, pred[]{:T(512)S(6)} %compare.3), kind=kOutput, calls=%fused_computation.13.clone.1 | convolution fusion | flops 809779200 | bytes 393221 | tf_op jit(solution)/shard_map/while/body/eval_jaxpr/gap,cgp->ac/dot_general | solution.py:162
  332.4 8.4 %fusion.105 = f32[16,512]{1,0:T(8,128)S(1)} fusion(s32[64,128]{1,0:T(8,128)S(1)} %dynamic-slice_bitcast_fusion.7, f32[64,128]{1,0:T(8,128)S(1)} %dynamic-slice_bitcast_fusion.8, bf16[16,64,16,128]{3,2,1,0:T(8,128)(2,1)} %get-tuple-element.220, s32[]{:T(128)S(6)} %copy.105, f32[16,512]{1,0:T(8,128)S(1)} %get-tuple-element.212, pred[]{:T(512)S(6)} %compare.3), kind=kOutput, calls=%fused_computation.13.clone.1 | convolution fusion | flops 809779200 | bytes 393221 | tf_op jit(solution)/shard_map/while/body/eval_jaxpr/gap,cgp->ac/dot_general | solution.py:162
  341.6 8.4 %fusion.105 = f32[16,512]{1,0:T(8,128)S(1)} fusion(s32[64,128]{1,0:T(8,128)S(1)} %dynamic-slice_bitcast_fusion.7, f32[64,128]{1,0:T(8,128)S(1)} %dynamic-slice_bitcast_fusion.8, bf16[16,64,16,128]{3,2,1,0:T(8,128)(2,1)} %get-tuple-element.220, s32[]{:T(128)S(6)} %copy.105, f32[16,512]{1,0:T(8,128)S(1)} %get-tuple-element.212, pred[]{:T(512)S(6)} %compare.3), kind=kOutput, calls=%fused_computation.13.clone.1 | convolution fusion | flops 809779200 | bytes 393221 | tf_op jit(solution)/shard_map/while/body/eval_jaxpr/gap,cgp->ac/dot_general | solution.py:162
  350.8 8.4 %fusion.105 = f32[16,512]{1,0:T(8,128)S(1)} fusion(s32[64,128]{1,0:T(8,128)S(1)} %dynamic-slice_bitcast_fusion.7, f32[64,128]{1,0:T(8,128)S(1)} %dynamic-slice_bitcast_fusion.8, bf16[16,64,16,128]{3,2,1,0:T(8,128)(2,1)} %get-tuple-element.220, s32[]{:T(128)S(6)} %copy.105, f32[16,512]{1,0:T(8,128)S(1)} %get-tuple-element.212, pred[]{:T(512)S(6)} %compare.3), kind=kOutput, calls=%fused_computation.13.clone.1 | convolution fusion | flops 809779200 | bytes 393221 | tf_op jit(solution)/shard_map/while/body/eval_jaxpr/gap,cgp->ac/dot_general | solution.py:162
  360.1 8.4 %fusion.105 = f32[16,512]{1,0:T(8,128)S(1)} fusion(s32[64,128]{1,0:T(8,128)S(1)} %dynamic-slice_bitcast_fusion.7, f32[64,128]{1,0:T(8,128)S(1)} %dynamic-slice_bitcast_fusion.8, bf16[16,64,16,128]{3,2,1,0:T(8,128)(2,1)} %get-tuple-element.220, s32[]{:T(128)S(6)} %copy.105, f32[16,512]{1,0:T(8,128)S(1)} %get-tuple-element.212, pred[]{:T(512)S(6)} %compare.3), kind=kOutput, calls=%fused_computation.13.clone.1 | convolution fusion | flops 809779200 | bytes 393221 | tf_op jit(solution)/shard_map/while/body/eval_jaxpr/gap,cgp->ac/dot_general | solution.py:162
  369.3 8.4 %fusion.105 = f32[16,512]{1,0:T(8,128)S(1)} fusion(s32[64,128]{1,0:T(8,128)S(1)} %dynamic-slice_bitcast_fusion.7, f32[64,128]{1,0:T(8,128)S(1)} %dynamic-slice_bitcast_fusion.8, bf16[16,64,16,128]{3,2,1,0:T(8,128)(2,1)} %get-tuple-element.220, s32[]{:T(128)S(6)} %copy.105, f32[16,512]{1,0:T(8,128)S(1)} %get-tuple-element.212, pred[]{:T(512)S(6)} %compare.3), kind=kOutput, calls=%fused_computation.13.clone.1 | convolution fusion | flops 809779200 | bytes 393221 | tf_op jit(solution)/shard_map/while/body/eval_jaxpr/gap,cgp->ac/dot_general | solution.py:162
  378.5 8.4 %fusion.105 = f32[16,512]{1,0:T(8,128)S(1)} fusion(s32[64,128]{1,0:T(8,128)S(1)} %dynamic-slice_bitcast_fusion.7, f32[64,128]{1,0:T(8,128)S(1)} %dynamic-slice_bitcast_fusion.8, bf16[16,64,16,128]{3,2,1,0:T(8,128)(2,1)} %get-tuple-element.220, s32[]{:T(128)S(6)} %copy.105, f32[16,512]{1,0:T(8,128)S(1)} %get-tuple-element.212, pred[]{:T(512)S(6)} %compare.3), kind=kOutput, calls=%fused_computation.13.clone.1 | convolution fusion | flops 809779200 | bytes 393221 | tf_op jit(solution)/shard_map/while/body/eval_jaxpr/gap,cgp->ac/dot_general | solution.py:162
  387.7 8.4 %fusion.105 = f32[16,512]{1,0:T(8,128)S(1)} fusion(s32[64,128]{1,0:T(8,128)S(1)} %dynamic-slice_bitcast_fusion.7, f32[64,128]{1,0:T(8,128)S(1)} %dynamic-slice_bitcast_fusion.8, bf16[16,64,16,128]{3,2,1,0:T(8,128)(2,1)} %get-tuple-element.220, s32[]{:T(128)S(6)} %copy.105, f32[16,512]{1,0:T(8,128)S(1)} %get-tuple-element.212, pred[]{:T(512)S(6)} %compare.3), kind=kOutput, calls=%fused_computation.13.clone.1 | convolution fusion | flops 809779200 | bytes 393221 | tf_op jit(solution)/shard_map/while/body/eval_jaxpr/gap,cgp->ac/dot_general | solution.py:162
  397.0 8.4 %fusion.105 = f32[16,512]{1,0:T(8,128)S(1)} fusion(s32[64,128]{1,0:T(8,128)S(1)} %dynamic-slice_bitcast_fusion.7, f32[64,128]{1,0:T(8,128)S(1)} %dynamic-slice_bitcast_fusion.8, bf16[16,64,16,128]{3,2,1,0:T(8,128)(2,1)} %get-tuple-element.220, s32[]{:T(128)S(6)} %copy.105, f32[16,512]{1,0:T(8,128)S(1)} %get-tuple-element.212, pred[]{:T(512)S(6)} %compare.3), kind=kOutput, calls=%fused_computation.13.clone.1 | convolution fusion | flops 809779200 | bytes 393221 | tf_op jit(solution)/shard_map/while/body/eval_jaxpr/gap,cgp->ac/dot_general | solution.py:162
  406.2 8.4 %fusion.105 = f32[16,512]{1,0:T(8,128)S(1)} fusion(s32[64,128]{1,0:T(8,128)S(1)} %dynamic-slice_bitcast_fusion.7, f32[64,128]{1,0:T(8,128)S(1)} %dynamic-slice_bitcast_fusion.8, bf16[16,64,16,128]{3,2,1,0:T(8,128)(2,1)} %get-tuple-element.220, s32[]{:T(128)S(6)} %copy.105, f32[16,512]{1,0:T(8,128)S(1)} %get-tuple-element.212, pred[]{:T(512)S(6)} %compare.3), kind=kOutput, calls=%fused_computation.13.clone.1 | convolution fusion | flops 809779200 | bytes 393221 | tf_op jit(solution)/shard_map/while/body/eval_jaxpr/gap,cgp->ac/dot_general | solution.py:162
  415.4 8.4 %fusion.105 = f32[16,512]{1,0:T(8,128)S(1)} fusion(s32[64,128]{1,0:T(8,128)S(1)} %dynamic-slice_bitcast_fusion.7, f32[64,128]{1,0:T(8,128)S(1)} %dynamic-slice_bitcast_fusion.8, bf16[16,64,16,128]{3,2,1,0:T(8,128)(2,1)} %get-tuple-element.220, s32[]{:T(128)S(6)} %copy.105, f32[16,512]{1,0:T(8,128)S(1)} %get-tuple-element.212, pred[]{:T(512)S(6)} %compare.3), kind=kOutput, calls=%fused_computation.13.clone.1 | convolution fusion | flops 809779200 | bytes 393221 | tf_op jit(solution)/shard_map/while/body/eval_jaxpr/gap,cgp->ac/dot_general | solution.py:162
  424.7 8.4 %fusion.105 = f32[16,512]{1,0:T(8,128)S(1)} fusion(s32[64,128]{1,0:T(8,128)S(1)} %dynamic-slice_bitcast_fusion.7, f32[64,128]{1,0:T(8,128)S(1)} %dynamic-slice_bitcast_fusion.8, bf16[16,64,16,128]{3,2,1,0:T(8,128)(2,1)} %get-tuple-element.220, s32[]{:T(128)S(6)} %copy.105, f32[16,512]{1,0:T(8,128)S(1)} %get-tuple-element.212, pred[]{:T(512)S(6)} %compare.3), kind=kOutput, calls=%fused_computation.13.clone.1 | convolution fusion | flops 809779200 | bytes 393221 | tf_op jit(solution)/shard_map/while/body/eval_jaxpr/gap,cgp->ac/dot_general | solution.py:162
  433.9 8.4 %fusion.105 = f32[16,512]{1,0:T(8,128)S(1)} fusion(s32[64,128]{1,0:T(8,128)S(1)} %dynamic-slice_bitcast_fusion.7, f32[64,128]{1,0:T(8,128)S(1)} %dynamic-slice_bitcast_fusion.8, bf16[16,64,16,128]{3,2,1,0:T(8,128)(2,1)} %get-tuple-element.220, s32[]{:T(128)S(6)} %copy.105, f32[16,512]{1,0:T(8,128)S(1)} %get-tuple-element.212, pred[]{:T(512)S(6)} %compare.3), kind=kOutput, calls=%fused_computation.13.clone.1 | convolution fusion | flops 809779200 | bytes 393221 | tf_op jit(solution)/shard_map/while/body/eval_jaxpr/gap,cgp->ac/dot_general | solution.py:162
  443.1 8.4 %fusion.105 = f32[16,512]{1,0:T(8,128)S(1)} fusion(s32[64,128]{1,0:T(8,128)S(1)} %dynamic-slice_bitcast_fusion.7, f32[64,128]{1,0:T(8,128)S(1)} %dynamic-slice_bitcast_fusion.8, bf16[16,64,16,128]{3,2,1,0:T(8,128)(2,1)} %get-tuple-element.220, s32[]{:T(128)S(6)} %copy.105, f32[16,512]{1,0:T(8,128)S(1)} %get-tuple-element.212, pred[]{:T(512)S(6)} %compare.3), kind=kOutput, calls=%fused_computation.13.clone.1 | convolution fusion | flops 809779200 | bytes 393221 | tf_op jit(solution)/shard_map/while/body/eval_jaxpr/gap,cgp->ac/dot_general | solution.py:162
  452.3 8.4 %fusion.105 = f32[16,512]{1,0:T(8,128)S(1)} fusion(s32[64,128]{1,0:T(8,128)S(1)} %dynamic-slice_bitcast_fusion.7, f32[64,128]{1,0:T(8,128)S(1)} %dynamic-slice_bitcast_fusion.8, bf16[16,64,16,128]{3,2,1,0:T(8,128)(2,1)} %get-tuple-element.220, s32[]{:T(128)S(6)} %copy.105, f32[16,512]{1,0:T(8,128)S(1)} %get-tuple-element.212, pred[]{:T(512)S(6)} %compare.3), kind=kOutput, calls=%fused_computation.13.clone.1 | convolution fusion | flops 809779200 | bytes 393221 | tf_op jit(solution)/shard_map/while/body/eval_jaxpr/gap,cgp->ac/dot_general | solution.py:162
  463.0 5.3 %collective-permute-start.2 = (f32[16,32,4]{2,0,1:T(8,128)S(1)}, f32[16,32,4]{2,0,1:T(8,128)}, u32[]{:S(2)}, u32[]{:S(2)}) collective-permute-start(f32[16,32,4]{2,0,1:T(8,128)S(1)} %get-tuple-element.105), channel_id=1, source_target_pairs={{0,4},{4,8},{8,12},{12,16},{16,20},{20,24},{24,28},{1,5},{5,9},{9,... | collective-permute-start | bytes 24584 | tf_op jit(solution)/shard_map/ppermute | solution.py:18
  470.8 5.7 %collective-permute-done.2 = f32[16,32,4]{2,0,1:T(8,128)} collective-permute-done((f32[16,32,4]{2,0,1:T(8,128)S(1)}, f32[16,32,4]{2,0,1:T(8,128)}, u32[]{:S(2)}, u32[]{:S(2)}) %collective-permute-start.2) | collective-permute-done | bytes 8224 | tf_op jit(solution)/shard_map/ppermute | solution.py:18
  476.5 10.4 %fusion.25 = bf16[16,32,512]{2,0,1:T(8,128)(2,1)} fusion(f32[16,32,512]{2,0,1:T(8,128)S(1)} %fusion.71, f32[16,32,4]{2,0,1:T(8,128)} %collective-permute-done.3, f32[16,32,4]{2,0,1:T(8,128)} %collective-permute-done.2, f32[16,1,32,512]{3,0,2,1:T(8,128)S(1)} %get-tuple-element.100, f32[]{:T(128)S(6)} %mul.235, f32[16,512]{1,0:T(8,128)S(1)} %get-tuple-element.60, ...), kind=kLoop, calls=%fused_computation.60 | loop fusion | flops 7077888 | bytes 2670628 | tf_op jit(solution)/shard_map/convert_element_type | solution.py:172
  486.9 23.0 %all-gather.5.cloned.1.call-done = bf16[64,32,512]{2,0,1:T(8,128)(2,1)} async-done(((bf16[16,32,512]{2,0,1:T(8,128)(2,1)}), bf16[64,32,512]{2,0,1:T(8,128)(2,1)}) %all-gather.5.cloned.1.call-update) | async-done | bytes 2097168 | tf_op jit(solution)/shard_map/all_gather | solution.py:177
  (129 shorter events, 82.8 us)
Async XLA Ops:
  6.5 13.2 %copy-start.9 = (bf16[512,16,128]{2,1,0:T(8,128)(2,1)S(1)}, bf16[512,16,128]{2,1,0:T(8,128)(2,1)}, u32[]{:S(2)}) copy-start(bf16[512,16,128]{2,1,0:T(8,128)(2,1)} %param.16) | copy-start | bytes 6291460
  11.5 1.0 copy-start.5
  12.4 21.8 %all-to-all-start.3 = ((s32[8,128,128]{1,2,0:T(8,128)}), s32[8,128,128]{1,2,0:T(8,128)S(1)}, u32[]{:S(2)}, u32[]{:S(2)}) async-start(s32[8,128,128]{1,2,0:T(8,128)} %copy_bitcast_fusion), calls=%async_computation.3 | async-start | bytes 1048576 | tf_op jit(solution)/shard_map/all_to_all | solution.py:136
  34.2 0.8 copy-start.2
  35.0 4.8 copy-start
  35.0 6.2 %copy-start.6 = (bf16[512,128]{1,0:T(8,128)(2,1)S(1)}, bf16[512,128]{1,0:T(8,128)(2,1)}, u32[]{:S(2)}) copy-start(bf16[512,128]{1,0:T(8,128)(2,1)} %param.18) | copy-start | bytes 393220
  35.0 99.3 %all-to-all-start = ((bf16[1024,16,128]{2,1,0:T(8,128)(2,1)}), bf16[1024,16,128]{2,1,0:T(8,128)(2,1)}, u32[]{:S(2)}, u32[]{:S(2)}) async-start(bf16[1024,16,128]{2,1,0:T(8,128)(2,1)} %bitcast.110), calls=%async_computation | async-start | bytes 8388608 | tf_op jit(solution)/shard_map/all_to_all | solution.py:132
  39.7 1.7 copy-start.7
  39.7 6.6 %copy-start.1 = (bf16[16,4,32,512]{3,2,1,0:T(8,128)(2,1)S(1)}, bf16[16,4,32,512]{3,2,1,0:T(8,128)(2,1)}, u32[]{:S(2)}) copy-start(bf16[16,4,32,512]{3,2,1,0:T(8,128)(2,1)} %param.14) | copy-start | bytes 6291460
  39.7 26.3 %all-gather.3.cloned.1.call-start = ((), (), s32[]{:S(2)}) async-start(), calls=%async_computation.4 | async-start | bytes 2621440 | tf_op jit(solution)/shard_map/all_gather | solution.py:91
  47.7 27.7 %copy-start.8 = (f32[4]{0:T(128)S(1)}, f32[4]{0:T(128)}, u32[]{:S(2)}) copy-start(f32[4]{0:T(128)} %param.15) | copy-start | bytes 52
  47.7 28.3 %copy-start.4 = (bf16[1024,256]{0,1:T(8,128)(2,1)S(1)}, bf16[1024,256]{0,1:T(8,128)(2,1)}, u32[]{:S(2)}) copy-start(bf16[1024,256]{0,1:T(8,128)(2,1)} %fusion.18) | copy-start | bytes 1572868
  47.7 29.4 %copy-start.3 = (s32[8,128,128]{1,2,0:T(8,128)S(1)}, s32[8,128,128]{1,2,0:T(8,128)}, u32[]{:S(2)}) copy-start(s32[8,128,128]{1,2,0:T(8,128)} %copy-done.2) | copy-start | bytes 1572868
  68.8 21.6 %collective-permute-start.1 = (f32[16,32,4]{2,0,1:T(8,128)}, f32[16,32,4]{2,0,1:T(8,128)}, u32[]{:S(2)}, u32[]{:S(2)}) collective-permute-start(f32[16,32,4]{2,0,1:T(8,128)} %get-tuple-element.108), channel_id=1, source_target_pairs={{4,0},{8,4},{12,8},{16,12},{20,16},{24,20},{28,24},{5,1},{9,5},{13... | collective-permute-start | bytes 24584 | tf_op jit(solution)/shard_map/ppermute | solution.py:19
  70.1 20.3 %collective-permute-start = (f32[16,32,4]{2,0,1:T(8,128)S(1)}, f32[16,32,4]{2,0,1:T(8,128)}, u32[]{:S(2)}, u32[]{:S(2)}) collective-permute-start(f32[16,32,4]{2,0,1:T(8,128)S(1)} %get-tuple-element.107), channel_id=1, source_target_pairs={{0,4},{4,8},{8,12},{12,16},{16,20},{20,24},{24,28},{1,5},{5,9},{9,... | collective-permute-start | bytes 24584 | tf_op jit(solution)/shard_map/ppermute | solution.py:18
  134.3 143.0 %all-to-all-start.2 = ((bf16[1024,2,128]{2,1,0:T(2,128)(2,1)}), bf16[1024,2,128]{2,1,0:T(2,128)(2,1)S(1)}, u32[]{:S(2)}, u32[]{:S(2)}) async-start(bf16[1024,2,128]{2,1,0:T(2,128)(2,1)} %copy.58), calls=%async_computation.2 | async-start | bytes 1048576 | tf_op jit(solution)/shard_map/all_to_all | solution.py:133
  153.7 158.0 %all-reduce.2.cloned.1.call-start = ((), (), s32[]{:S(2)}) async-start(), calls=%async_computation.5 | async-start | bytes 1048576 | tf_op jit(solution)/shard_map/psum | solution.py:153
  277.3 12.2 %all-to-all-start.1 = ((s32[8,128,1]{1,2,0:T(1,128)}), s32[8,128,1]{1,2,0:T(1,128)S(1)}, u32[]{:S(2)}, u32[]{:S(2)}) async-start(s32[8,128,1]{1,2,0:T(1,128)} %slice_bitcast_fusion.1), calls=%async_computation.1 | async-start | bytes 8192 | tf_op jit(solution)/shard_map/all_to_all | solution.py:137
  283.1 226.8 %all-gather.5.cloned.1.call-start = ((), (), s32[]{:S(2)}) async-start(), calls=%async_computation.6 | async-start | bytes 2621440 | tf_op jit(solution)/shard_map/all_gather | solution.py:177
  461.8 9.1 %collective-permute-start.3 = (f32[16,32,4]{2,0,1:T(8,128)}, f32[16,32,4]{2,0,1:T(8,128)}, u32[]{:S(2)}, u32[]{:S(2)}) collective-permute-start(f32[16,32,4]{2,0,1:T(8,128)} %get-tuple-element.106), channel_id=1, source_target_pairs={{4,0},{8,4},{12,8},{16,12},{20,16},{24,20},{28,24},{5,1},{9,5},{13... | collective-permute-start | bytes 24584 | tf_op jit(solution)/shard_map/ppermute | solution.py:19
  463.0 13.4 %collective-permute-start.2 = (f32[16,32,4]{2,0,1:T(8,128)S(1)}, f32[16,32,4]{2,0,1:T(8,128)}, u32[]{:S(2)}, u32[]{:S(2)}) collective-permute-start(f32[16,32,4]{2,0,1:T(8,128)S(1)} %get-tuple-element.105), channel_id=1, source_target_pairs={{0,4},{4,8},{8,12},{12,16},{16,20},{20,24},{24,28},{1,5},{5,9},{9,... | collective-permute-start | bytes 24584 | tf_op jit(solution)/shard_map/ppermute | solution.py:18
Sparse Core Ops, SparseCore 0:
  42.1 23.8 all-gather.2
  277.4 34.3 all-reduce.1
  487.0 22.7 all-gather.4
where the time goes:
time: 525 us; the launch traced here: 520 us
  matrix products  248 us (47%)
  waiting for transfers between devices  128 us (24%)
  local copies, waits for them, and re-layouts  51.6 us (10%)
  starting transfers between devices  50.5 us (10%)
  other arithmetic  28.7 us (5%)
  between operations  14 us (3%)
    dot_general x16, matrix products, adjoint_group(): jnp.einsum('gap,cgp->ac', contrib, onehot, precision=lax.Precision.HIGHEST)  135 us
    dot_general x16, matrix products, forward_group(): jnp.einsum('ac,cgp->gap', column_field, onehot, precision=lax.Precision.H...  101 us
    all_to_all x1, waiting for transfers between devices, body(): lax.all_to_all(kernel_buf, 'horiz', split_axis=0, concat_axis=0, tiled=True)  30.8 us
    eq x32, local copies, waits for them, and re-layouts, column_onehot(): jnp.arange(col_count, dtype=jnp.int32)[:, None, None]  24.7 us
    all_gather x1, waiting for transfers between devices, body(): lax.all_gather(smoothed_b, 'lev', axis=0, tiled=True)  23 us
    psum x1, waiting for transfers between devices, body(): evolved = lax.psum(local_sums, 'lev')  22.2 us
    all_to_all x1, starting transfers between devices, body(): lax.all_to_all(value_buf, 'horiz', split_axis=0, concat_axis=0, tiled=True)  19.4 us
    all_gather x1, waiting for transfers between devices, body(): lax.all_gather(control_b, 'lev', axis=0, tiled=True)  18.3 us
  transfers between devices with their start and end apart: 11, of which 9 were waited for; matrix products, arithmetic and copies ran while one was open for 30% of the time, Pallas kernels for 0%

commit v1 on v0

--- a/solution.py
+++ b/solution.py
@@ -150,7 +150,7 @@
     local_sums = lax.map(forward_group, (kernel_groups, column_groups)).reshape(
         total_slots, pixel_width
     )
-    evolved = lax.psum(local_sums, "lev")
+    evolved = jnp.sum(lax.all_gather(local_sums, "lev"), axis=0)
     misfit = pixel_misfit(evolved, value_in[:, 0], value_in[:, 1], count_in)
     misfit_groups = misfit.reshape(group_count, slot_group, pixel_width)
 

time: 525 us -> 531 us (1.011)
  local copies, waits for them, and re-layouts: 51.6 us -> 64 us
  waiting for transfers between devices: 128 us -> 120 us
    psum x1 -> x0, waiting for transfers between devices: 22.2 us -> none  [body(): evolved = lax.psum(local_sums, 'lev')]
    all_to_all x1, starting transfers between devices: 19.4 us -> 3.49 us  [body(): lax.all_to_all(value_buf, 'horiz', split_axis=0, concat_axis=0, tiled=True)]
    all_to_all x1, starting transfers between devices: 5.77 us -> 19.5 us  [body(): lax.all_to_all(count_buf, 'horiz', split_axis=0, concat_axis=0, tiled=True)]
    mul x16, local copies, waits for them, and re-layouts: 0.05 us -> 12.2 us  [adjoint_group(): contrib = kernel_block.astype(jnp.float32) * misfit_block[:, None, :]]
    all_to_all x1, waiting for transfers between devices: 0.01 us -> 11.8 us  [body(): lax.all_to_all(value_buf, 'horiz', split_axis=0, concat_axis=0, tiled=True)]
  transfers between devices with their start and end apart: 11 -> 11, of which waited for: 9 -> 9; matrix products, arithmetic and copies ran while one was open for 30% -> 6% of each run, Pallas kernels for 0% -> 0%
where the time goes in v1:
time: 531 us; the launch traced here: 526 us
  matrix products  247 us (47%)
  waiting for transfers between devices  120 us (23%)
  local copies, waits for them, and re-layouts  64 us (12%)
  starting transfers between devices  48.4 us (9%)
  other arithmetic  32.6 us (6%)
  between operations  14 us (3%)
    dot_general x16, matrix products, adjoint_group(): jnp.einsum('gap,cgp->ac', contrib, onehot, precision=lax.Precision.HIGHEST)  135 us
    dot_general x16, matrix products, forward_group(): jnp.einsum('ac,cgp->gap', column_field, onehot, precision=lax.Precision.H...  101 us
    all_to_all x1, waiting for transfers between devices, body(): lax.all_to_all(kernel_buf, 'horiz', split_axis=0, concat_axis=0, tiled=True)  32.6 us
    eq x32, local copies, waits for them, and re-layouts, column_onehot(): jnp.arange(col_count, dtype=jnp.int32)[:, None, None]  24.8 us
    all_gather x1, waiting for transfers between devices, body(): lax.all_gather(smoothed_b, 'lev', axis=0, tiled=True)  22 us
    all_gather x1, waiting for transfers between devices, body(): lax.all_gather(control_b, 'lev', axis=0, tiled=True)  21.4 us
    all_to_all x1, starting transfers between devices, body(): lax.all_to_all(count_buf, 'horiz', split_axis=0, concat_axis=0, tiled=True)  19.5 us
    ppermute x2, waiting for transfers between devices, with_halo(): after = lax.ppermute(first, axis, down)  13.7 us
  transfers between devices with their start and end apart: 11, of which 9 were waited for; matrix products, arithmetic and copies ran while one was open for 6% of the time, Pallas kernels for 0%

profile of v1, /device:TPU:0, one launch (start us, length us, event | category | flops | bytes accessed | tf_op | source)
XLA Modules:
  0.0 525.9 jit_solution(14433081305617840344)
XLA Ops:
  12.4 7.3 %all-to-all-start.3 = ((s32[8,128,128]{1,2,0:T(8,128)}), s32[8,128,128]{1,2,0:T(8,128)S(1)}, u32[]{:S(2)}, u32[]{:S(2)}) async-start(s32[8,128,128]{1,2,0:T(8,128)} %copy_bitcast_fusion), calls=%async_computation.3 | async-start | bytes 1048576 | tf_op jit(solution)/shard_map/all_to_all | solution.py:136
  25.5 8.7 %all-to-all-done.3 = s32[8,128,128]{1,2,0:T(8,128)S(1)} async-done(((s32[8,128,128]{1,2,0:T(8,128)}), s32[8,128,128]{1,2,0:T(8,128)S(1)}, u32[]{:S(2)}, u32[]{:S(2)}) %all-to-all-start.3) | async-done | bytes 524320 | tf_op jit(solution)/shard_map/all_to_all | solution.py:136
  35.0 4.7 all-to-all-start
  44.6 21.4 %all-gather.4.cloned.1.call-done = bf16[64,32,512]{2,0,1:T(8,128)(2,1)} async-done(((bf16[16,32,512]{2,0,1:T(8,128)(2,1)}), bf16[64,32,512]{2,0,1:T(8,128)(2,1)}) %all-gather.4.cloned.1.call-update) | async-done | bytes 2097168 | tf_op jit(solution)/shard_map/all_gather | solution.py:91
  69.5 5.3 collective-permute-start
  76.5 12.1 %collective-permute-done.1 = f32[16,32,4]{2,0,1:T(8,128)S(1)} collective-permute-done((f32[16,32,4]{2,0,1:T(8,128)S(1)}, f32[16,32,4]{2,0,1:T(8,128)S(1)}, u32[]{:S(2)}, u32[]{:S(2)}) %collective-permute-start.1) | collective-permute-done | bytes 8224 | tf_op jit(solution)/shard_map/ppermute | solution.py:19
  88.6 13.1 %fusion.47 = (f32[16,512]{1,0:T(8,128)S(1)}, f32[16,1,32,512]{3,0,2,1:T(8,128)S(1)}) fusion(f32[16,32,512]{2,0,1:T(8,128)S(1)} %fusion.83, f32[16,32,4]{2,0,1:T(8,128)S(1)} %collective-permute-done.1, f32[16,32,4]{2,0,1:T(8,128)} %collective-permute-done, f32[]{:T(128)} %bitcast.31, f32[]{:T(128)} %bitcast.30, f32[]{:T(128)} %bitcast.29, f32[]{:T(128)} %bitcast.28, ...), kind=kLoop, calls=%fused_computation.82 | loop fusion | flops 9953280 | bytes 4243508 | tf_op jit(solution)/shard_map/reduce_sum | solution.py:98
  101.7 32.6 %all-to-all-done = bf16[1024,16,128]{2,1,0:T(8,128)(2,1)} async-done(((bf16[1024,16,128]{2,1,0:T(8,128)(2,1)}), bf16[1024,16,128]{2,1,0:T(8,128)(2,1)}, u32[]{:S(2)}, u32[]{:S(2)}) %all-to-all-start) | async-done | bytes 4194336 | tf_op jit(solution)/shard_map/all_to_all | solution.py:132
  134.3 123.5 %while.23 = (s32[]{:T(128)}, f32[16,64,128]{2,1,0:T(8,128)}, bf16[16,64,16,128]{3,2,1,0:T(8,128)(2,1)}, s32[16,64,128]{2,1,0:T(8,128)}, f32[16,512]{1,0:T(8,128)S(1)}) while((s32[]{:T(128)}, f32[16,64,128]{2,1,0:T(8,128)}, bf16[16,64,16,128]{3,2,1,0:T(8,128)(2,1)}, s32[16,64,128]{2,1,0:T(8,128)}, f32[16,512]{1,0:T(8,128)S(1)}) %tuple.71), condition=%wide.region_5.6_spmd.clone, body=%wide.region_3.5_spmd.sunk.clone | while | flops 809885696 | bytes 491601 | solution.py:150
  135.1 6.3 %fusion.107 = f32[64,128]{1,0:T(8,128)S(1)} fusion(s32[64,128]{1,0:T(8,128)S(1)} %dynamic-slice_bitcast_fusion.9, bf16[16,64,16,128]{3,2,1,0:T(8,128)(2,1)} %get-tuple-element.223, s32[]{:T(128)S(6)} %copy.92, f32[16,512]{1,0:T(8,128)S(1)} %get-tuple-element.225), kind=kOutput, calls=%fused_computation.5.clone.1.clone | convolution fusion | flops 809885696 | bytes 360452 | tf_op jit(solution)/shard_map/while/body/eval_jaxpr/ac,cgp->gap/dot_general | solution.py:147
  142.8 6.3 %fusion.107 = f32[64,128]{1,0:T(8,128)S(1)} fusion(s32[64,128]{1,0:T(8,128)S(1)} %dynamic-slice_bitcast_fusion.9, bf16[16,64,16,128]{3,2,1,0:T(8,128)(2,1)} %get-tuple-element.223, s32[]{:T(128)S(6)} %copy.92, f32[16,512]{1,0:T(8,128)S(1)} %get-tuple-element.225), kind=kOutput, calls=%fused_computation.5.clone.1.clone | convolution fusion | flops 809885696 | bytes 360452 | tf_op jit(solution)/shard_map/while/body/eval_jaxpr/ac,cgp->gap/dot_general | solution.py:147
  150.6 6.3 %fusion.107 = f32[64,128]{1,0:T(8,128)S(1)} fusion(s32[64,128]{1,0:T(8,128)S(1)} %dynamic-slice_bitcast_fusion.9, bf16[16,64,16,128]{3,2,1,0:T(8,128)(2,1)} %get-tuple-element.223, s32[]{:T(128)S(6)} %copy.92, f32[16,512]{1,0:T(8,128)S(1)} %get-tuple-element.225), kind=kOutput, calls=%fused_computation.5.clone.1.clone | convolution fusion | flops 809885696 | bytes 360452 | tf_op jit(solution)/shard_map/while/body/eval_jaxpr/ac,cgp->gap/dot_general | solution.py:147
  158.3 6.3 %fusion.107 = f32[64,128]{1,0:T(8,128)S(1)} fusion(s32[64,128]{1,0:T(8,128)S(1)} %dynamic-slice_bitcast_fusion.9, bf16[16,64,16,128]{3,2,1,0:T(8,128)(2,1)} %get-tuple-element.223, s32[]{:T(128)S(6)} %copy.92, f32[16,512]{1,0:T(8,128)S(1)} %get-tuple-element.225), kind=kOutput, calls=%fused_computation.5.clone.1.clone | convolution fusion | flops 809885696 | bytes 360452 | tf_op jit(solution)/shard_map/while/body/eval_jaxpr/ac,cgp->gap/dot_general | solution.py:147
  166.0 6.3 %fusion.107 = f32[64,128]{1,0:T(8,128)S(1)} fusion(s32[64,128]{1,0:T(8,128)S(1)} %dynamic-slice_bitcast_fusion.9, bf16[16,64,16,128]{3,2,1,0:T(8,128)(2,1)} %get-tuple-element.223, s32[]{:T(128)S(6)} %copy.92, f32[16,512]{1,0:T(8,128)S(1)} %get-tuple-element.225), kind=kOutput, calls=%fused_computation.5.clone.1.clone | convolution fusion | flops 809885696 | bytes 360452 | tf_op jit(solution)/shard_map/while/body/eval_jaxpr/ac,cgp->gap/dot_general | solution.py:147
  173.7 6.3 %fusion.107 = f32[64,128]{1,0:T(8,128)S(1)} fusion(s32[64,128]{1,0:T(8,128)S(1)} %dynamic-slice_bitcast_fusion.9, bf16[16,64,16,128]{3,2,1,0:T(8,128)(2,1)} %get-tuple-element.223, s32[]{:T(128)S(6)} %copy.92, f32[16,512]{1,0:T(8,128)S(1)} %get-tuple-element.225), kind=kOutput, calls=%fused_computation.5.clone.1.clone | convolution fusion | flops 809885696 | bytes 360452 | tf_op jit(solution)/shard_map/while/body/eval_jaxpr/ac,cgp->gap/dot_general | solution.py:147
  181.4 6.3 %fusion.107 = f32[64,128]{1,0:T(8,128)S(1)} fusion(s32[64,128]{1,0:T(8,128)S(1)} %dynamic-slice_bitcast_fusion.9, bf16[16,64,16,128]{3,2,1,0:T(8,128)(2,1)} %get-tuple-element.223, s32[]{:T(128)S(6)} %copy.92, f32[16,512]{1,0:T(8,128)S(1)} %get-tuple-element.225), kind=kOutput, calls=%fused_computation.5.clone.1.clone | convolution fusion | flops 809885696 | bytes 360452 | tf_op jit(solution)/shard_map/while/body/eval_jaxpr/ac,cgp->gap/dot_general | solution.py:147
  189.1 6.3 %fusion.107 = f32[64,128]{1,0:T(8,128)S(1)} fusion(s32[64,128]{1,0:T(8,128)S(1)} %dynamic-slice_bitcast_fusion.9, bf16[16,64,16,128]{3,2,1,0:T(8,128)(2,1)} %get-tuple-element.223, s32[]{:T(128)S(6)} %copy.92, f32[16,512]{1,0:T(8,128)S(1)} %get-tuple-element.225), kind=kOutput, calls=%fused_computation.5.clone.1.clone | convolution fusion | flops 809885696 | bytes 360452 | tf_op jit(solution)/shard_map/while/body/eval_jaxpr/ac,cgp->gap/dot_general | solution.py:147
  196.8 6.3 %fusion.107 = f32[64,128]{1,0:T(8,128)S(1)} fusion(s32[64,128]{1,0:T(8,128)S(1)} %dynamic-slice_bitcast_fusion.9, bf16[16,64,16,128]{3,2,1,0:T(8,128)(2,1)} %get-tuple-element.223, s32[]{:T(128)S(6)} %copy.92, f32[16,512]{1,0:T(8,128)S(1)} %get-tuple-element.225), kind=kOutput, calls=%fused_computation.5.clone.1.clone | convolution fusion | flops 809885696 | bytes 360452 | tf_op jit(solution)/shard_map/while/body/eval_jaxpr/ac,cgp->gap/dot_general | solution.py:147
  204.6 6.3 %fusion.107 = f32[64,128]{1,0:T(8,128)S(1)} fusion(s32[64,128]{1,0:T(8,128)S(1)} %dynamic-slice_bitcast_fusion.9, bf16[16,64,16,128]{3,2,1,0:T(8,128)(2,1)} %get-tuple-element.223, s32[]{:T(128)S(6)} %copy.92, f32[16,512]{1,0:T(8,128)S(1)} %get-tuple-element.225), kind=kOutput, calls=%fused_computation.5.clone.1.clone | convolution fusion | flops 809885696 | bytes 360452 | tf_op jit(solution)/shard_map/while/body/eval_jaxpr/ac,cgp->gap/dot_general | solution.py:147
  212.3 6.3 %fusion.107 = f32[64,128]{1,0:T(8,128)S(1)} fusion(s32[64,128]{1,0:T(8,128)S(1)} %dynamic-slice_bitcast_fusion.9, bf16[16,64,16,128]{3,2,1,0:T(8,128)(2,1)} %get-tuple-element.223, s32[]{:T(128)S(6)} %copy.92, f32[16,512]{1,0:T(8,128)S(1)} %get-tuple-element.225), kind=kOutput, calls=%fused_computation.5.clone.1.clone | convolution fusion | flops 809885696 | bytes 360452 | tf_op jit(solution)/shard_map/while/body/eval_jaxpr/ac,cgp->gap/dot_general | solution.py:147
  220.0 6.3 %fusion.107 = f32[64,128]{1,0:T(8,128)S(1)} fusion(s32[64,128]{1,0:T(8,128)S(1)} %dynamic-slice_bitcast_fusion.9, bf16[16,64,16,128]{3,2,1,0:T(8,128)(2,1)} %get-tuple-element.223, s32[]{:T(128)S(6)} %copy.92, f32[16,512]{1,0:T(8,128)S(1)} %get-tuple-element.225), kind=kOutput, calls=%fused_computation.5.clone.1.clone | convolution fusion | flops 809885696 | bytes 360452 | tf_op jit(solution)/shard_map/while/body/eval_jaxpr/ac,cgp->gap/dot_general | solution.py:147
  227.7 6.3 %fusion.107 = f32[64,128]{1,0:T(8,128)S(1)} fusion(s32[64,128]{1,0:T(8,128)S(1)} %dynamic-slice_bitcast_fusion.9, bf16[16,64,16,128]{3,2,1,0:T(8,128)(2,1)} %get-tuple-element.223, s32[]{:T(128)S(6)} %copy.92, f32[16,512]{1,0:T(8,128)S(1)} %get-tuple-element.225), kind=kOutput, calls=%fused_computation.5.clone.1.clone | convolution fusion | flops 809885696 | bytes 360452 | tf_op jit(solution)/shard_map/while/body/eval_jaxpr/ac,cgp->gap/dot_general | solution.py:147
  235.4 6.3 %fusion.107 = f32[64,128]{1,0:T(8,128)S(1)} fusion(s32[64,128]{1,0:T(8,128)S(1)} %dynamic-slice_bitcast_fusion.9, bf16[16,64,16,128]{3,2,1,0:T(8,128)(2,1)} %get-tuple-element.223, s32[]{:T(128)S(6)} %copy.92, f32[16,512]{1,0:T(8,128)S(1)} %get-tuple-element.225), kind=kOutput, calls=%fused_computation.5.clone.1.clone | convolution fusion | flops 809885696 | bytes 360452 | tf_op jit(solution)/shard_map/while/body/eval_jaxpr/ac,cgp->gap/dot_general | solution.py:147
  243.1 6.3 %fusion.107 = f32[64,128]{1,0:T(8,128)S(1)} fusion(s32[64,128]{1,0:T(8,128)S(1)} %dynamic-slice_bitcast_fusion.9, bf16[16,64,16,128]{3,2,1,0:T(8,128)(2,1)} %get-tuple-element.223, s32[]{:T(128)S(6)} %copy.92, f32[16,512]{1,0:T(8,128)S(1)} %get-tuple-element.225), kind=kOutput, calls=%fused_computation.5.clone.1.clone | convolution fusion | flops 809885696 | bytes 360452 | tf_op jit(solution)/shard_map/while/body/eval_jaxpr/ac,cgp->gap/dot_general | solution.py:147
  250.8 6.3 %fusion.107 = f32[64,128]{1,0:T(8,128)S(1)} fusion(s32[64,128]{1,0:T(8,128)S(1)} %dynamic-slice_bitcast_fusion.9, bf16[16,64,16,128]{3,2,1,0:T(8,128)(2,1)} %get-tuple-element.223, s32[]{:T(128)S(6)} %copy.92, f32[16,512]{1,0:T(8,128)S(1)} %get-tuple-element.225), kind=kOutput, calls=%fused_computation.5.clone.1.clone | convolution fusion | flops 809885696 | bytes 360452 | tf_op jit(solution)/shard_map/while/body/eval_jaxpr/ac,cgp->gap/dot_general | solution.py:147
  259.2 19.5 %all-to-all-start.1 = ((s32[8,128,1]{1,2,0:T(1,128)}), s32[8,128,1]{1,2,0:T(1,128)S(1)}, u32[]{:S(2)}, u32[]{:S(2)}) async-start(s32[8,128,1]{1,2,0:T(1,128)} %slice_bitcast_fusion.1), calls=%async_computation.1 | async-start | bytes 8192 | tf_op jit(solution)/shard_map/all_to_all | solution.py:137
  290.3 11.8 %all-to-all-done.2 = bf16[1024,2,128]{2,1,0:T(2,128)(2,1)S(1)} async-done(((bf16[1024,2,128]{2,1,0:T(2,128)(2,1)}), bf16[1024,2,128]{2,1,0:T(2,128)(2,1)S(1)}, u32[]{:S(2)}, u32[]{:S(2)}) %all-to-all-start.2) | async-done | bytes 524320 | tf_op jit(solution)/shard_map/all_to_all | solution.py:133
  308.2 159.7 %while.24 = (s32[]{:T(128)}, f32[16,512]{1,0:T(8,128)S(1)}, bf16[16,64,16,128]{3,2,1,0:T(8,128)(2,1)}, f32[16,64,128]{2,1,0:T(8,128)}, s32[16,64,128]{2,1,0:T(8,128)}) while((s32[]{:T(128)}, f32[16,512]{1,0:T(8,128)S(1)}, bf16[16,64,16,128]{3,2,1,0:T(8,128)(2,1)}, f32[16,64,128]{2,1,0:T(8,128)}, ...), condition=%wide.region_8.9_spmd.clone.clone, body=%wide.region_7.8_spmd.clone.sunk.clone | while | flops 809779200 | bytes 524379 | solution.py:166
  309.7 8.4 %fusion.108 = f32[16,512]{1,0:T(8,128)S(1)} fusion(s32[64,128]{1,0:T(8,128)S(1)} %dynamic-slice_bitcast_fusion.10, f32[64,128]{1,0:T(8,128)S(1)} %dynamic-slice_bitcast_fusion.11, bf16[16,64,16,128]{3,2,1,0:T(8,128)(2,1)} %get-tuple-element.238, s32[]{:T(128)S(6)} %copy.98, f32[16,512]{1,0:T(8,128)S(1)} %get-tuple-element.232, pred[]{:T(512)S(6)} %compare.4), kind=kOutput, calls=%fused_computation.13.clone.1.clone | convolution fusion | flops 809779200 | bytes 393221 | tf_op jit(solution)/shard_map/while/body/eval_jaxpr/gap,cgp->ac/dot_general | solution.py:162
  319.7 8.4 %fusion.108 = f32[16,512]{1,0:T(8,128)S(1)} fusion(s32[64,128]{1,0:T(8,128)S(1)} %dynamic-slice_bitcast_fusion.10, f32[64,128]{1,0:T(8,128)S(1)} %dynamic-slice_bitcast_fusion.11, bf16[16,64,16,128]{3,2,1,0:T(8,128)(2,1)} %get-tuple-element.238, s32[]{:T(128)S(6)} %copy.98, f32[16,512]{1,0:T(8,128)S(1)} %get-tuple-element.232, pred[]{:T(512)S(6)} %compare.4), kind=kOutput, calls=%fused_computation.13.clone.1.clone | convolution fusion | flops 809779200 | bytes 393221 | tf_op jit(solution)/shard_map/while/body/eval_jaxpr/gap,cgp->ac/dot_general | solution.py:162
  329.7 8.4 %fusion.108 = f32[16,512]{1,0:T(8,128)S(1)} fusion(s32[64,128]{1,0:T(8,128)S(1)} %dynamic-slice_bitcast_fusion.10, f32[64,128]{1,0:T(8,128)S(1)} %dynamic-slice_bitcast_fusion.11, bf16[16,64,16,128]{3,2,1,0:T(8,128)(2,1)} %get-tuple-element.238, s32[]{:T(128)S(6)} %copy.98, f32[16,512]{1,0:T(8,128)S(1)} %get-tuple-element.232, pred[]{:T(512)S(6)} %compare.4), kind=kOutput, calls=%fused_computation.13.clone.1.clone | convolution fusion | flops 809779200 | bytes 393221 | tf_op jit(solution)/shard_map/while/body/eval_jaxpr/gap,cgp->ac/dot_general | solution.py:162
  339.7 8.4 %fusion.108 = f32[16,512]{1,0:T(8,128)S(1)} fusion(s32[64,128]{1,0:T(8,128)S(1)} %dynamic-slice_bitcast_fusion.10, f32[64,128]{1,0:T(8,128)S(1)} %dynamic-slice_bitcast_fusion.11, bf16[16,64,16,128]{3,2,1,0:T(8,128)(2,1)} %get-tuple-element.238, s32[]{:T(128)S(6)} %copy.98, f32[16,512]{1,0:T(8,128)S(1)} %get-tuple-element.232, pred[]{:T(512)S(6)} %compare.4), kind=kOutput, calls=%fused_computation.13.clone.1.clone | convolution fusion | flops 809779200 | bytes 393221 | tf_op jit(solution)/shard_map/while/body/eval_jaxpr/gap,cgp->ac/dot_general | solution.py:162
  349.7 8.4 %fusion.108 = f32[16,512]{1,0:T(8,128)S(1)} fusion(s32[64,128]{1,0:T(8,128)S(1)} %dynamic-slice_bitcast_fusion.10, f32[64,128]{1,0:T(8,128)S(1)} %dynamic-slice_bitcast_fusion.11, bf16[16,64,16,128]{3,2,1,0:T(8,128)(2,1)} %get-tuple-element.238, s32[]{:T(128)S(6)} %copy.98, f32[16,512]{1,0:T(8,128)S(1)} %get-tuple-element.232, pred[]{:T(512)S(6)} %compare.4), kind=kOutput, calls=%fused_computation.13.clone.1.clone | convolution fusion | flops 809779200 | bytes 393221 | tf_op jit(solution)/shard_map/while/body/eval_jaxpr/gap,cgp->ac/dot_general | solution.py:162
  359.7 8.4 %fusion.108 = f32[16,512]{1,0:T(8,128)S(1)} fusion(s32[64,128]{1,0:T(8,128)S(1)} %dynamic-slice_bitcast_fusion.10, f32[64,128]{1,0:T(8,128)S(1)} %dynamic-slice_bitcast_fusion.11, bf16[16,64,16,128]{3,2,1,0:T(8,128)(2,1)} %get-tuple-element.238, s32[]{:T(128)S(6)} %copy.98, f32[16,512]{1,0:T(8,128)S(1)} %get-tuple-element.232, pred[]{:T(512)S(6)} %compare.4), kind=kOutput, calls=%fused_computation.13.clone.1.clone | convolution fusion | flops 809779200 | bytes 393221 | tf_op jit(solution)/shard_map/while/body/eval_jaxpr/gap,cgp->ac/dot_general | solution.py:162
  369.6 8.4 %fusion.108 = f32[16,512]{1,0:T(8,128)S(1)} fusion(s32[64,128]{1,0:T(8,128)S(1)} %dynamic-slice_bitcast_fusion.10, f32[64,128]{1,0:T(8,128)S(1)} %dynamic-slice_bitcast_fusion.11, bf16[16,64,16,128]{3,2,1,0:T(8,128)(2,1)} %get-tuple-element.238, s32[]{:T(128)S(6)} %copy.98, f32[16,512]{1,0:T(8,128)S(1)} %get-tuple-element.232, pred[]{:T(512)S(6)} %compare.4), kind=kOutput, calls=%fused_computation.13.clone.1.clone | convolution fusion | flops 809779200 | bytes 393221 | tf_op jit(solution)/shard_map/while/body/eval_jaxpr/gap,cgp->ac/dot_general | solution.py:162
  379.6 8.4 %fusion.108 = f32[16,512]{1,0:T(8,128)S(1)} fusion(s32[64,128]{1,0:T(8,128)S(1)} %dynamic-slice_bitcast_fusion.10, f32[64,128]{1,0:T(8,128)S(1)} %dynamic-slice_bitcast_fusion.11, bf16[16,64,16,128]{3,2,1,0:T(8,128)(2,1)} %get-tuple-element.238, s32[]{:T(128)S(6)} %copy.98, f32[16,512]{1,0:T(8,128)S(1)} %get-tuple-element.232, pred[]{:T(512)S(6)} %compare.4), kind=kOutput, calls=%fused_computation.13.clone.1.clone | convolution fusion | flops 809779200 | bytes 393221 | tf_op jit(solution)/shard_map/while/body/eval_jaxpr/gap,cgp->ac/dot_general | solution.py:162
  389.6 8.4 %fusion.108 = f32[16,512]{1,0:T(8,128)S(1)} fusion(s32[64,128]{1,0:T(8,128)S(1)} %dynamic-slice_bitcast_fusion.10, f32[64,128]{1,0:T(8,128)S(1)} %dynamic-slice_bitcast_fusion.11, bf16[16,64,16,128]{3,2,1,0:T(8,128)(2,1)} %get-tuple-element.238, s32[]{:T(128)S(6)} %copy.98, f32[16,512]{1,0:T(8,128)S(1)} %get-tuple-element.232, pred[]{:T(512)S(6)} %compare.4), kind=kOutput, calls=%fused_computation.13.clone.1.clone | convolution fusion | flops 809779200 | bytes 393221 | tf_op jit(solution)/shard_map/while/body/eval_jaxpr/gap,cgp->ac/dot_general | solution.py:162
  399.6 8.4 %fusion.108 = f32[16,512]{1,0:T(8,128)S(1)} fusion(s32[64,128]{1,0:T(8,128)S(1)} %dynamic-slice_bitcast_fusion.10, f32[64,128]{1,0:T(8,128)S(1)} %dynamic-slice_bitcast_fusion.11, bf16[16,64,16,128]{3,2,1,0:T(8,128)(2,1)} %get-tuple-element.238, s32[]{:T(128)S(6)} %copy.98, f32[16,512]{1,0:T(8,128)S(1)} %get-tuple-element.232, pred[]{:T(512)S(6)} %compare.4), kind=kOutput, calls=%fused_computation.13.clone.1.clone | convolution fusion | flops 809779200 | bytes 393221 | tf_op jit(solution)/shard_map/while/body/eval_jaxpr/gap,cgp->ac/dot_general | solution.py:162
  409.6 8.4 %fusion.108 = f32[16,512]{1,0:T(8,128)S(1)} fusion(s32[64,128]{1,0:T(8,128)S(1)} %dynamic-slice_bitcast_fusion.10, f32[64,128]{1,0:T(8,128)S(1)} %dynamic-slice_bitcast_fusion.11, bf16[16,64,16,128]{3,2,1,0:T(8,128)(2,1)} %get-tuple-element.238, s32[]{:T(128)S(6)} %copy.98, f32[16,512]{1,0:T(8,128)S(1)} %get-tuple-element.232, pred[]{:T(512)S(6)} %compare.4), kind=kOutput, calls=%fused_computation.13.clone.1.clone | convolution fusion | flops 809779200 | bytes 393221 | tf_op jit(solution)/shard_map/while/body/eval_jaxpr/gap,cgp->ac/dot_general | solution.py:162
  419.6 8.4 %fusion.108 = f32[16,512]{1,0:T(8,128)S(1)} fusion(s32[64,128]{1,0:T(8,128)S(1)} %dynamic-slice_bitcast_fusion.10, f32[64,128]{1,0:T(8,128)S(1)} %dynamic-slice_bitcast_fusion.11, bf16[16,64,16,128]{3,2,1,0:T(8,128)(2,1)} %get-tuple-element.238, s32[]{:T(128)S(6)} %copy.98, f32[16,512]{1,0:T(8,128)S(1)} %get-tuple-element.232, pred[]{:T(512)S(6)} %compare.4), kind=kOutput, calls=%fused_computation.13.clone.1.clone | convolution fusion | flops 809779200 | bytes 393221 | tf_op jit(solution)/shard_map/while/body/eval_jaxpr/gap,cgp->ac/dot_general | solution.py:162
  429.5 8.4 %fusion.108 = f32[16,512]{1,0:T(8,128)S(1)} fusion(s32[64,128]{1,0:T(8,128)S(1)} %dynamic-slice_bitcast_fusion.10, f32[64,128]{1,0:T(8,128)S(1)} %dynamic-slice_bitcast_fusion.11, bf16[16,64,16,128]{3,2,1,0:T(8,128)(2,1)} %get-tuple-element.238, s32[]{:T(128)S(6)} %copy.98, f32[16,512]{1,0:T(8,128)S(1)} %get-tuple-element.232, pred[]{:T(512)S(6)} %compare.4), kind=kOutput, calls=%fused_computation.13.clone.1.clone | convolution fusion | flops 809779200 | bytes 393221 | tf_op jit(solution)/shard_map/while/body/eval_jaxpr/gap,cgp->ac/dot_general | solution.py:162
  439.5 8.4 %fusion.108 = f32[16,512]{1,0:T(8,128)S(1)} fusion(s32[64,128]{1,0:T(8,128)S(1)} %dynamic-slice_bitcast_fusion.10, f32[64,128]{1,0:T(8,128)S(1)} %dynamic-slice_bitcast_fusion.11, bf16[16,64,16,128]{3,2,1,0:T(8,128)(2,1)} %get-tuple-element.238, s32[]{:T(128)S(6)} %copy.98, f32[16,512]{1,0:T(8,128)S(1)} %get-tuple-element.232, pred[]{:T(512)S(6)} %compare.4), kind=kOutput, calls=%fused_computation.13.clone.1.clone | convolution fusion | flops 809779200 | bytes 393221 | tf_op jit(solution)/shard_map/while/body/eval_jaxpr/gap,cgp->ac/dot_general | solution.py:162
  449.5 8.4 %fusion.108 = f32[16,512]{1,0:T(8,128)S(1)} fusion(s32[64,128]{1,0:T(8,128)S(1)} %dynamic-slice_bitcast_fusion.10, f32[64,128]{1,0:T(8,128)S(1)} %dynamic-slice_bitcast_fusion.11, bf16[16,64,16,128]{3,2,1,0:T(8,128)(2,1)} %get-tuple-element.238, s32[]{:T(128)S(6)} %copy.98, f32[16,512]{1,0:T(8,128)S(1)} %get-tuple-element.232, pred[]{:T(512)S(6)} %compare.4), kind=kOutput, calls=%fused_computation.13.clone.1.clone | convolution fusion | flops 809779200 | bytes 393221 | tf_op jit(solution)/shard_map/while/body/eval_jaxpr/gap,cgp->ac/dot_general | solution.py:162
  459.5 8.4 %fusion.108 = f32[16,512]{1,0:T(8,128)S(1)} fusion(s32[64,128]{1,0:T(8,128)S(1)} %dynamic-slice_bitcast_fusion.10, f32[64,128]{1,0:T(8,128)S(1)} %dynamic-slice_bitcast_fusion.11, bf16[16,64,16,128]{3,2,1,0:T(8,128)(2,1)} %get-tuple-element.238, s32[]{:T(128)S(6)} %copy.98, f32[16,512]{1,0:T(8,128)S(1)} %get-tuple-element.232, pred[]{:T(512)S(6)} %compare.4), kind=kOutput, calls=%fused_computation.13.clone.1.clone | convolution fusion | flops 809779200 | bytes 393221 | tf_op jit(solution)/shard_map/while/body/eval_jaxpr/gap,cgp->ac/dot_general | solution.py:162
  470.2 5.3 collective-permute-start.2
  477.7 5.1 collective-permute-done.2
  482.8 10.5 %fusion.25 = bf16[16,32,512]{2,0,1:T(8,128)(2,1)} fusion(f32[16,32,512]{2,0,1:T(8,128)S(1)} %fusion.71, f32[16,32,4]{2,0,1:T(8,128)} %collective-permute-done.3, f32[16,32,4]{2,0,1:T(8,128)} %collective-permute-done.2, f32[16,1,32,512]{3,0,2,1:T(8,128)S(1)} %get-tuple-element.100, f32[]{:T(128)S(6)} %mul.236, f32[16,512]{1,0:T(8,128)S(1)} %get-tuple-element.60, ...), kind=kLoop, calls=%fused_computation.60 | loop fusion | flops 7077888 | bytes 2670628 | tf_op jit(solution)/shard_map/convert_element_type | solution.py:172
  493.3 22.0 %all-gather.8.cloned.1.call-done = bf16[64,32,512]{2,0,1:T(8,128)(2,1)} async-done(((bf16[16,32,512]{2,0,1:T(8,128)(2,1)}), bf16[64,32,512]{2,0,1:T(8,128)(2,1)}) %all-gather.8.cloned.1.call-update) | async-done | bytes 2097168 | tf_op jit(solution)/shard_map/all_gather | solution.py:177
  (133 shorter events, 96.2 us)
Async XLA Ops:
  6.5 13.2 %copy-start.9 = (bf16[512,16,128]{2,1,0:T(8,128)(2,1)S(1)}, bf16[512,16,128]{2,1,0:T(8,128)(2,1)}, u32[]{:S(2)}) copy-start(bf16[512,16,128]{2,1,0:T(8,128)(2,1)} %param.16) | copy-start | bytes 6291460
  11.5 1.0 copy-start.5
  12.4 21.8 %all-to-all-start.3 = ((s32[8,128,128]{1,2,0:T(8,128)}), s32[8,128,128]{1,2,0:T(8,128)S(1)}, u32[]{:S(2)}, u32[]{:S(2)}) async-start(s32[8,128,128]{1,2,0:T(8,128)} %copy_bitcast_fusion), calls=%async_computation.3 | async-start | bytes 1048576 | tf_op jit(solution)/shard_map/all_to_all | solution.py:136
  34.2 0.8 copy-start.2
  35.0 4.8 copy-start
  35.0 99.3 %all-to-all-start = ((bf16[1024,16,128]{2,1,0:T(8,128)(2,1)}), bf16[1024,16,128]{2,1,0:T(8,128)(2,1)}, u32[]{:S(2)}, u32[]{:S(2)}) async-start(bf16[1024,16,128]{2,1,0:T(8,128)(2,1)} %bitcast.123), calls=%async_computation | async-start | bytes 8388608 | tf_op jit(solution)/shard_map/all_to_all | solution.py:132
  39.7 3.4 copy-start.1
  39.7 26.3 %all-gather.4.cloned.1.call-start = ((), (), s32[]{:S(2)}) async-start(), calls=%async_computation.4 | async-start | bytes 2621440 | tf_op jit(solution)/shard_map/all_gather | solution.py:91
  41.2 262.4 %all-gather.6.cloned.1.call-start = ((), (), s32[]{:S(2)}) async-start(), calls=%async_computation.5 | async-start | bytes 2621440 | tf_op jit(solution)/shard_map/all_gather | solution.py:153
  44.6 30.1 %copy-start.8 = (f32[4]{0:T(128)S(1)}, f32[4]{0:T(128)}, u32[]{:S(2)}) copy-start(f32[4]{0:T(128)} %param.15) | copy-start | bytes 52
  44.6 30.8 %copy-start.3 = (s32[8,128,128]{1,2,0:T(8,128)S(1)}, s32[8,128,128]{1,2,0:T(8,128)}, u32[]{:S(2)}) copy-start(s32[8,128,128]{1,2,0:T(8,128)} %copy-done.2) | copy-start | bytes 1572868
  68.2 20.4 %collective-permute-start.1 = (f32[16,32,4]{2,0,1:T(8,128)S(1)}, f32[16,32,4]{2,0,1:T(8,128)S(1)}, u32[]{:S(2)}, u32[]{:S(2)}) collective-permute-start(f32[16,32,4]{2,0,1:T(8,128)S(1)} %get-tuple-element.108), channel_id=1, source_target_pairs={{4,0},{8,4},{12,8},{16,12},{20,16},{24,20},{28,24},{5,1},{9,5},{13... | collective-permute-start | bytes 24584 | tf_op jit(solution)/shard_map/ppermute | solution.py:19
  69.5 19.1 %collective-permute-start = (f32[16,32,4]{2,0,1:T(8,128)S(1)}, f32[16,32,4]{2,0,1:T(8,128)}, u32[]{:S(2)}, u32[]{:S(2)}) collective-permute-start(f32[16,32,4]{2,0,1:T(8,128)S(1)} %get-tuple-element.107), channel_id=1, source_target_pairs={{0,4},{4,8},{8,12},{12,16},{16,20},{20,24},{24,28},{1,5},{5,9},{9,... | collective-permute-start | bytes 24584 | tf_op jit(solution)/shard_map/ppermute | solution.py:18
  134.3 144.3 %copy-start.6 = (bf16[512,128]{1,0:T(8,128)(2,1)S(1)}, bf16[512,128]{1,0:T(8,128)(2,1)}, u32[]{:S(2)}) copy-start(bf16[512,128]{1,0:T(8,128)(2,1)} %param.18) | copy-start | bytes 393220
  134.3 144.5 %copy-start.7 = (bf16[512,128]{1,0:T(8,128)(2,1)S(1)}, bf16[512,128]{1,0:T(8,128)(2,1)}, u32[]{:S(2)}) copy-start(bf16[512,128]{1,0:T(8,128)(2,1)} %param.17) | copy-start | bytes 393220
  259.2 26.0 %all-to-all-start.1 = ((s32[8,128,1]{1,2,0:T(1,128)}), s32[8,128,1]{1,2,0:T(1,128)S(1)}, u32[]{:S(2)}, u32[]{:S(2)}) async-start(s32[8,128,1]{1,2,0:T(1,128)} %slice_bitcast_fusion.1), calls=%async_computation.1 | async-start | bytes 8192 | tf_op jit(solution)/shard_map/all_to_all | solution.py:137
  285.1 16.9 %all-to-all-start.2 = ((bf16[1024,2,128]{2,1,0:T(2,128)(2,1)}), bf16[1024,2,128]{2,1,0:T(2,128)(2,1)S(1)}, u32[]{:S(2)}, u32[]{:S(2)}) async-start(bf16[1024,2,128]{2,1,0:T(2,128)(2,1)} %copy.57), calls=%async_computation.2 | async-start | bytes 1048576 | tf_op jit(solution)/shard_map/all_to_all | solution.py:133
  288.6 226.7 %all-gather.8.cloned.1.call-start = ((), (), s32[]{:S(2)}) async-start(), calls=%async_computation.6 | async-start | bytes 2621440 | tf_op jit(solution)/shard_map/all_gather | solution.py:177
  303.6 2.6 copy-start.4
  468.9 8.7 %collective-permute-start.3 = (f32[16,32,4]{2,0,1:T(8,128)}, f32[16,32,4]{2,0,1:T(8,128)}, u32[]{:S(2)}, u32[]{:S(2)}) collective-permute-start(f32[16,32,4]{2,0,1:T(8,128)} %get-tuple-element.106), channel_id=1, source_target_pairs={{4,0},{8,4},{12,8},{16,12},{20,16},{24,20},{28,24},{5,1},{9,5},{13... | collective-permute-start | bytes 24584 | tf_op jit(solution)/shard_map/ppermute | solution.py:19
  470.2 12.6 %collective-permute-start.2 = (f32[16,32,4]{2,0,1:T(8,128)S(1)}, f32[16,32,4]{2,0,1:T(8,128)}, u32[]{:S(2)}, u32[]{:S(2)}) collective-permute-start(f32[16,32,4]{2,0,1:T(8,128)S(1)} %get-tuple-element.105), channel_id=1, source_target_pairs={{0,4},{4,8},{8,12},{12,16},{16,20},{20,24},{24,28},{1,5},{5,9},{9,... | collective-permute-start | bytes 24584 | tf_op jit(solution)/shard_map/ppermute | solution.py:18
Sparse Core Ops, SparseCore 0:
  42.1 23.8 all-gather.3
  257.9 37.5 all-gather.5
  493.4 21.8 all-gather.7
